TPU v7x, 512 devices: a whole 4x8x8 slice. The times are simulated.
512 devices in a mesh: dp: 8 (over x, core), ctx: 64 (over y, z).
Axes of the slice: x: 4, y: 8, z: 8, core: 2. Of those that a mesh axis runs over, the one named last changes fastest.
Arguments:
- token_ids: int32 [8, 8192], P('dp', 'ctx'), may hold values from 0 to 7
- queries: bfloat16 [8, 8192, 4096], P('dp', 'ctx'), may hold values from -6 to 6
- gated_values: bfloat16 [8, 8192, 4096], P('dp', 'ctx'), may hold values from -6 to 6
- out_grad: bfloat16 [8, 8192, 4096], P('dp', 'ctx'), may hold values from -6 to 6
- filters: bfloat16 [4096, 128], P('ctx'), may hold values from -0.5 to 0.5
Outputs:
- value_grad: bfloat16 [8, 8192, 4096], P('dp', 'ctx')
- filter_grad: float32 [4096, 128], P('ctx')
Inputs may be any that keep to these rules, and one draw needn't show every extreme that they name: `token_ids`: ids 0 to 3 are upper-case bases, 4 to 7 lower-case bases.
All inputs are finite; a program needn't handle non-finite values.
Results may differ from a plain program's by a relative error of at most 0.0049.
Values may be sent and summed in bfloat16 or wider, within the bound.
A program may use at most 64 MiB of HBM per device.

v0:
```python
import jax
import jax.numpy as jnp
import numpy as np
from jax import lax
from jax.sharding import PartitionSpec as P


def tables(span):
    half = span // 2
    angle = np.pi * (2 * np.arange(half)[:, None] + 1) * np.arange(span)[None, :] / span
    wave = np.concatenate([np.cos(angle), np.sin(angle)], axis=0)
    high = wave.astype(jnp.bfloat16)
    low = (wave - high.astype(np.float64)).astype(jnp.bfloat16)
    return (high, low)


def mul(a, b):
    return jnp.dot(a, b, preferred_element_type=jnp.float32)


def body(token_ids, queries, gated_values, out_grad, filters):
    dp, ctx = (lax.axis_size("dp"), lax.axis_size("ctx"))
    weight = jnp.where(token_ids < 4, 1.0, 0.1).astype(jnp.float32)
    cotangent = (
        weight[:, :, None] * out_grad.astype(jnp.float32) * queries.astype(jnp.float32)
    ).astype(jnp.bfloat16)[0]
    rows = cotangent.shape[0]
    factor_tok = float(dp * ctx * rows) ** (-0.5)
    taps = lax.all_gather(filters, "ctx", axis=0, tiled=True)
    after = lax.ppermute(cotangent, "ctx", [(i, i - 1) for i in range(1, ctx)])
    high, low = (jnp.asarray(t) for t in tables(2 * rows))

    def forward(x):
        n = x.shape[0]
        wave = mul(high[:, :n], x) + mul(low[:, :n], x)
        return (wave[:rows], wave[rows:])

    def backward(re, im):
        both = jnp.concatenate([re, im], axis=0) * (1.0 / rows)
        top = both.astype(jnp.bfloat16)
        rest = (both - top.astype(jnp.float32)).astype(jnp.bfloat16)
        up, down = (high[:, :rows].T, low[:, :rows].T)
        return mul(up, top) + (mul(up, rest) + mul(down, top))

    cot_cos, cot_sin = forward(jnp.concatenate([cotangent, after], axis=0))

    def correlate(x):
        x_cos, x_sin = forward(x)
        return backward(cot_cos * x_cos + cot_sin * x_sin, cot_sin * x_cos - cot_cos * x_sin)

    tap_part = correlate(gated_values[0]).T * factor_tok
    filter_grad = lax.psum(lax.psum_scatter(tap_part, "ctx", scatter_dimension=0, tiled=True), "dp")
    value_grad = correlate(taps.T).astype(jnp.bfloat16)[None]
    return (value_grad, filter_grad)


def solution(mesh):
    return jax.shard_map(
        body,
        mesh=mesh,
        in_specs=(
            P("dp", "ctx"),
            P("dp", "ctx", None),
            P("dp", "ctx", None),
            P("dp", "ctx", None),
            P("ctx", None),
        ),
        out_specs=(P("dp", "ctx", None), P("ctx", None)),
        check_vma=False,
    )
```

profile of v0, /device:TPU:16, one launch (start us, length us, event | category | flops | bytes accessed | tf_op | source)
XLA Modules:
  0.0 386.2 jit_solution(3704554985823753769)
XLA Ops:
  7.2 0.0 copy-start
  7.2 0.0 copy-start.5
  7.2 0.0 all-gather.2.cloned.1.call-start
  7.2 0.7 all-gather.2.cloned.1.call-update
  7.9 0.0 reduce-scatter.2.cloned.1.call-start
  8.0 0.7 fusion.25
  8.6 1.9 fusion.13
  10.6 0.0 copy-start.4
  10.6 11.0 %collective-permute-start = (bf16[128,4096]{1,0:T(8,128)(2,1)S(1)}, bf16[128,4096]{1,0:T(8,128)(2,1)S(1)}, u32[]{:S(2)}, u32[]{:S(2)}) collective-permute-start(bf16[128,4096]{1,0:T(8,128)(2,1)S(1)} %fusion.13), channel_id=1, source_target_pairs={{1,0},{2,1},{3,2},{4,3},{5,4},{6,5},{7,6},{8,7},{9,8},{10,9},{11,1... | collective-permute-start | bytes 3145736 | tf_op jit(solution)/shard_map/ppermute | solution.py:30
  21.6 0.0 copy-done.5
  21.6 0.7 fusion.40
  22.3 0.0 copy-done.4
  22.3 0.7 fusion.39
  23.0 0.0 copy-done
  23.0 0.7 fusion.15
  23.7 0.0 copy-start.7
  23.7 2.7 convolution_add_fusion.2
  26.4 0.0 copy-start.6
  26.4 17.9 %collective-permute-done = bf16[128,4096]{1,0:T(8,128)(2,1)S(1)} collective-permute-done((bf16[128,4096]{1,0:T(8,128)(2,1)S(1)}, bf16[128,4096]{1,0:T(8,128)(2,1)S(1)}, u32[]{:S(2)}, u32[]{:S(2)}) %collective-permute-start) | collective-permute-done | bytes 1048608 | tf_op jit(solution)/shard_map/ppermute | solution.py:30
  44.3 0.0 copy-done.7
  44.3 0.7 convolution_add_fusion.1
  45.0 0.0 copy-done.6
  45.0 2.7 fusion.1
  47.7 49.9 %all-gather.2.cloned.1.call-done = bf16[4096,128]{1,0:T(8,128)(2,1)} async-done(((bf16[64,128]{1,0:T(8,128)(2,1)}), bf16[4096,128]{1,0:T(8,128)(2,1)}) %all-gather.2.cloned.1.call-update) | async-done | bytes 1048592 | tf_op jit(solution)/shard_map/all_gather | solution.py:29
  97.6 0.0 copy-start.3
  97.6 2.0 fusion.38
  99.6 0.0 copy-done.3
  99.6 0.0 copy-start.2
  99.6 2.7 convolution_add_fusion.3
  102.4 0.7 copy-done.2
  103.1 6.1 %multiply_add_fusion = (f32[128,4096]{1,0:T(8,128)S(1)}, f32[128,4096]{1,0:T(8,128)S(1)}, f32[128,4096]{1,0:T(8,128)S(1)}, f32[128,4096]{1,0:T(8,128)}) fusion(f32[256,4096]{1,0:T(8,128)S(1)} %copy-done.2, f32[256,4096]{1,0:T(8,128)} %fusion.1, f32[256,4096]{1,0:T(8,128)} %convolution_add_fusion.3), kind=kLoop, calls=%fused_computation.22 | loop fusion | flops 6291456 | bytes 20971520 | tf_op jit(solution)/shard_map/add | solution.py:49
  109.2 0.8 fusion.10
  110.0 0.8 fusion.23
  110.7 2.1 fusion.3
  112.8 0.0 reduce-scatter.2.cloned.1.call-update
  112.9 0.0 copy-start.1
  112.9 2.5 fusion.9
  115.4 0.0 copy-done.1
  115.4 0.8 fusion.19
  116.2 1.9 fusion.6
  118.1 2.3 copy.9
  120.4 234.3 %reduce-scatter.2.cloned.1.call-done = f32[64,128]{1,0:T(8,128)} async-done(((f32[4096,128]{1,0:T(8,128)}), f32[64,128]{1,0:T(8,128)}) %reduce-scatter.2.cloned.1.call-update) | async-done | bytes 32784 | tf_op jit(solution)/shard_map/reduce_scatter | solution.py:52
  354.7 24.7 %psum.7 = f32[64,128]{1,0:T(8,128)} all-reduce(f32[64,128]{1,0:T(8,128)} %reduce-scatter.2.cloned.1.call-done), channel_id=1, replica_groups=mesh['dp'=8,'ctx'=64] {'dp'}, use_global_device_ids=true, to_apply=%region_1.2 | all-reduce | flops 8192 | bytes 65536 | tf_op jit(solution)/shard_map/psum | solution.py:52
Async XLA Ops:
  7.2 15.8 %copy-start = (bf16[1,128,4096]{2,1,0:T(8,128)(2,1)S(1)}, bf16[1,128,4096]{2,1,0:T(8,128)(2,1)}, u32[]{:S(2)}) copy-start(bf16[1,128,4096]{2,1,0:T(8,128)(2,1)} %param.9) | copy-start | bytes 3145732
  7.2 14.4 %copy-start.5 = (bf16[256,128]{1,0:T(8,128)(2,1)S(1)}, bf16[256,128]{1,0:T(8,128)(2,1)}, u32[]{:S(2)}) copy-start(bf16[256,128]{1,0:T(8,128)(2,1)} %constant.22) | copy-start | bytes 196612
  7.2 90.4 %all-gather.2.cloned.1.call-start = ((), (), s32[]{:S(2)}) async-start(), calls=%async_computation.1 | async-start | bytes 1064960 | tf_op jit(solution)/shard_map/all_gather | solution.py:29
  7.9 346.8 %reduce-scatter.2.cloned.1.call-start = ((), (), s32[]{:S(2)}) async-start(), calls=%async_computation.2 | async-start | bytes 2129920 | tf_op jit(solution)/shard_map/reduce_scatter | solution.py:52
  10.6 11.7 %copy-start.4 = (bf16[256,128]{1,0:T(8,128)(2,1)S(1)}, bf16[256,128]{1,0:T(8,128)(2,1)}, u32[]{:S(2)}) copy-start(bf16[256,128]{1,0:T(8,128)(2,1)} %constant.20) | copy-start | bytes 196612
  10.6 33.7 %collective-permute-start = (bf16[128,4096]{1,0:T(8,128)(2,1)S(1)}, bf16[128,4096]{1,0:T(8,128)(2,1)S(1)}, u32[]{:S(2)}, u32[]{:S(2)}) collective-permute-start(bf16[128,4096]{1,0:T(8,128)(2,1)S(1)} %fusion.13), channel_id=1, source_target_pairs={{1,0},{2,1},{3,2},{4,3},{5,4},{6,5},{7,6},{8,7},{9,8},{10,9},{11,1... | collective-permute-start | bytes 3145736 | tf_op jit(solution)/shard_map/ppermute | solution.py:30
  23.7 20.6 %copy-start.7 = (bf16[256,128]{1,0:T(8,128)(2,1)S(1)}, bf16[256,128]{1,0:T(8,128)(2,1)}, u32[]{:S(2)}) copy-start(bf16[256,128]{1,0:T(8,128)(2,1)} %constant.21) | copy-start | bytes 196612
  26.4 18.6 %copy-start.6 = (bf16[256,128]{1,0:T(8,128)(2,1)S(1)}, bf16[256,128]{1,0:T(8,128)(2,1)}, u32[]{:S(2)}) copy-start(bf16[256,128]{1,0:T(8,128)(2,1)} %constant.23) | copy-start | bytes 196612
  97.6 2.0 copy-start.3
  99.6 3.5 copy-start.2
  112.9 2.5 copy-start.1
Sparse Core Ops, SparseCore 0:
  11.0 86.4 all-gather.1
  113.0 241.6 reduce-scatter.1
where the time goes:
time: 387 us; the launch traced here: 386 us
  waiting for transfers between devices  303 us (78%)
  blocking collectives  24.7 us (6%)
  matrix products  21.8 us (6%)
  between operations  14.2 us (4%)
  starting transfers between devices  11 us (3%)
  other arithmetic  8.73 us (2%)
    reduce_scatter x1, waiting for transfers between devices, body(): lax.psum_scatter(tap_part, 'ctx', scatter_dimension=0, tiled=True)  234 us
    all_gather x1, waiting for transfers between devices, body(): taps = lax.all_gather(filters, 'ctx', axis=0, tiled=True)  49.9 us
    psum x1, blocking collectives, body(): lax.psum(lax.psum_scatter(tap_part, 'ctx', scatter_dimension=0, tiled=Tru...  24.7 us
    dot_general x14, matrix products, mul(): return jnp.dot(a, b, preferred_element_type=jnp.float32)  21.8 us
    ppermute x1, waiting for transfers between devices, body(): after = lax.ppermute(cotangent, 'ctx', [(i, i - 1) for i in range(1, ctx)])  17.9 us
    ppermute x1, starting transfers between devices, body(): after = lax.ppermute(cotangent, 'ctx', [(i, i - 1) for i in range(1, ctx)])  11 us
  transfers between devices with their start and end apart: 3, of which 3 were waited for; matrix products, arithmetic and copies ran while one was open for 5% of the time, Pallas kernels for 0%

commit v1 on v0

--- a/solution.py
+++ b/solution.py
@@ -26,7 +26,12 @@
     ).astype(jnp.bfloat16)[0]
     rows = cotangent.shape[0]
     factor_tok = float(dp * ctx * rows) ** (-0.5)
-    taps = lax.all_gather(filters, "ctx", axis=0, tiled=True)
+    taps = jnp.concatenate(
+        lax.all_to_all(
+            jnp.stack(tuple((filters for _ in range(lax.axis_size("ctx")))), axis=0), "ctx", 0, 0
+        ),
+        axis=0,
+    )
     after = lax.ppermute(cotangent, "ctx", [(i, i - 1) for i in range(1, ctx)])
     high, low = (jnp.asarray(t) for t in tables(2 * rows))
 

time: 387 us -> 366 us (0.946)
  waiting for transfers between devices: 303 us -> 272 us
  starting transfers between devices: 11 us -> 21.2 us
    all_gather x1 -> x0, waiting for transfers between devices: 49.9 us -> none  [body(): taps = lax.all_gather(filters, 'ctx', axis=0, tiled=True)]
    ppermute x1, waiting for transfers between devices: 17.9 us -> 35.1 us  [body(): after = lax.ppermute(cotangent, 'ctx', [(i, i - 1) for i in range(1, ctx)])]
    all_to_all x0 -> x1, starting transfers between devices: none -> 16.5 us  [body(): lax.all_to_all(jnp.stack(tuple((filters for _ in range(lax.axis_size('ctx...]
    ppermute x1, starting transfers between devices: 11 us -> 4.71 us  [body(): after = lax.ppermute(cotangent, 'ctx', [(i, i - 1) for i in range(1, ctx)])]
  transfers between devices with their start and end apart: 3 -> 3, of which waited for: 3 -> 2; matrix products, arithmetic and copies ran while one was open for 5% -> 5% of each run, Pallas kernels for 0% -> 0%
where the time goes in v1:
time: 366 us; the launch traced here: 365 us
  waiting for transfers between devices  272 us (74%)
  blocking collectives  24.7 us (7%)
  starting transfers between devices  21.2 us (6%)
  matrix products  20.5 us (6%)
  between operations  14.2 us (4%)
  other arithmetic  7.79 us (2%)
  local copies, waits for them, and re-layouts  5.08 us (1%)
    reduce_scatter x1, waiting for transfers between devices, body(): lax.psum_scatter(tap_part, 'ctx', scatter_dimension=0, tiled=True)  237 us
    ppermute x1, waiting for transfers between devices, body(): after = lax.ppermute(cotangent, 'ctx', [(i, i - 1) for i in range(1, ctx)])  35.1 us
    psum x1, blocking collectives, body(): lax.psum(lax.psum_scatter(tap_part, 'ctx', scatter_dimension=0, tiled=Tru...  24.7 us
    dot_general x14, matrix products, mul(): return jnp.dot(a, b, preferred_element_type=jnp.float32)  20.5 us
    all_to_all x1, starting transfers between devices, body(): lax.all_to_all(jnp.stack(tuple((filters for _ in range(lax.axis_size('ctx...  16.5 us
  transfers between devices with their start and end apart: 3, of which 2 were waited for; matrix products, arithmetic and copies ran while one was open for 5% of the time, Pallas kernels for 0%

profile of v1, /device:TPU:16, one launch (start us, length us, event | category | flops | bytes accessed | tf_op | source)
XLA Modules:
  0.0 365.5 jit_solution(6006528147043479035)
XLA Ops:
  7.2 0.0 copy-start
  7.2 0.0 copy-start.8
  7.2 0.0 copy-start.5
  7.2 2.1 stack.2
  9.3 16.5 %all-to-all-start = ((bf16[64,64,128]{2,1,0:T(8,128)(2,1)}), bf16[64,64,128]{2,1,0:T(8,128)(2,1)S(1)}, u32[]{:S(2)}, u32[]{:S(2)}) async-start(bf16[64,64,128]{2,1,0:T(8,128)(2,1)} %stack.2), calls=%async_computation | async-start | bytes 2097152 | tf_op jit(solution)/shard_map/all_to_all | solution.py:30
  25.8 0.0 copy-start.4
  25.8 0.0 reduce-scatter.2.cloned.1.call-start
  25.8 0.0 copy-done.8
  25.9 0.0 copy-done.5
  25.9 1.6 fusion.13
  27.5 0.0 copy-start.3
  27.5 4.7 %collective-permute-start = (bf16[128,4096]{1,0:T(8,128)(2,1)S(1)}, bf16[128,4096]{1,0:T(8,128)(2,1)S(1)}, u32[]{:S(2)}, u32[]{:S(2)}) collective-permute-start(bf16[128,4096]{1,0:T(8,128)(2,1)S(1)} %fusion.13), channel_id=1, source_target_pairs={{1,0},{2,1},{3,2},{4,3},{5,4},{6,5},{7,6},{8,7},{9,8},{10,9},{11,1... | collective-permute-start | bytes 3145736 | tf_op jit(solution)/shard_map/ppermute | solution.py:35
  32.2 0.0 copy-done.4
  32.2 0.7 fusion.40
  32.9 0.0 copy-done.3
  33.0 0.7 fusion.39
  33.7 0.0 copy-done
  33.7 0.7 fusion.15
  34.4 0.0 copy-start.7
  34.4 2.7 convolution_add_fusion.2
  37.1 0.0 copy-start.6
  37.1 35.1 %collective-permute-done = bf16[128,4096]{1,0:T(8,128)(2,1)S(1)} collective-permute-done((bf16[128,4096]{1,0:T(8,128)(2,1)S(1)}, bf16[128,4096]{1,0:T(8,128)(2,1)S(1)}, u32[]{:S(2)}, u32[]{:S(2)}) %collective-permute-start) | collective-permute-done | bytes 1048608 | tf_op jit(solution)/shard_map/ppermute | solution.py:35
  72.1 0.0 copy-done.7
  72.1 0.7 convolution_add_fusion.1
  72.9 0.0 copy-done.6
  72.9 2.7 fusion.1
  75.6 0.0 all-to-all-done
  75.6 0.7 fusion.38
  76.3 0.0 copy-start.2
  76.3 2.7 convolution_add_fusion.3
  79.0 0.7 copy-done.2
  79.7 6.2 %multiply_add_fusion = (f32[128,4096]{1,0:T(8,128)S(1)}, f32[128,4096]{1,0:T(8,128)S(1)}, f32[128,4096]{1,0:T(8,128)S(1)}, f32[128,4096]{1,0:T(8,128)}) fusion(f32[256,4096]{1,0:T(8,128)S(1)} %copy-done.2, f32[256,4096]{1,0:T(8,128)} %fusion.1, f32[256,4096]{1,0:T(8,128)} %convolution_add_fusion.3), kind=kLoop, calls=%fused_computation.22 | loop fusion | flops 6291456 | bytes 20971520 | tf_op jit(solution)/shard_map/add | solution.py:54
  85.9 0.8 fusion.10
  86.6 0.8 fusion.23
  87.4 2.1 fusion.3
  89.5 0.0 reduce-scatter.2.cloned.1.call-update
  89.5 0.0 copy-start.1
  89.5 2.5 fusion.9
  92.0 0.0 copy-done.1
  92.1 0.8 fusion.19
  92.9 1.9 fusion.6
  94.8 2.3 copy.9
  97.1 236.8 %reduce-scatter.2.cloned.1.call-done = f32[64,128]{1,0:T(8,128)} async-done(((f32[4096,128]{1,0:T(8,128)}), f32[64,128]{1,0:T(8,128)}) %reduce-scatter.2.cloned.1.call-update) | async-done | bytes 32784 | tf_op jit(solution)/shard_map/reduce_scatter | solution.py:57
  333.9 24.7 %psum.7 = f32[64,128]{1,0:T(8,128)} all-reduce(f32[64,128]{1,0:T(8,128)} %reduce-scatter.2.cloned.1.call-done), channel_id=1, replica_groups=mesh['dp'=8,'ctx'=64] {'dp'}, use_global_device_ids=true, to_apply=%region_1.2 | all-reduce | flops 8192 | bytes 65536 | tf_op jit(solution)/shard_map/psum | solution.py:57
  (1 shorter events, 0.0 us)
Async XLA Ops:
  7.2 26.5 %copy-start = (bf16[1,128,4096]{2,1,0:T(8,128)(2,1)S(1)}, bf16[1,128,4096]{2,1,0:T(8,128)(2,1)}, u32[]{:S(2)}) copy-start(bf16[1,128,4096]{2,1,0:T(8,128)(2,1)} %param.9) | copy-start | bytes 3145732
  7.2 18.7 %copy-start.8 = (s32[1,128]{1,0:T(1,128)S(1)}, s32[1,128]{1,0:T(1,128)}, u32[]{:S(2)}) copy-start(s32[1,128]{1,0:T(1,128)} %param.7) | copy-start | bytes 1540
  7.2 18.7 %copy-start.5 = (bf16[1,128,4096]{2,1,0:T(8,128)(2,1)S(1)}, bf16[1,128,4096]{2,1,0:T(8,128)(2,1)}, u32[]{:S(2)}) copy-start(bf16[1,128,4096]{2,1,0:T(8,128)(2,1)} %param.8) | copy-start | bytes 3145732
  9.3 66.3 %all-to-all-start = ((bf16[64,64,128]{2,1,0:T(8,128)(2,1)}), bf16[64,64,128]{2,1,0:T(8,128)(2,1)S(1)}, u32[]{:S(2)}, u32[]{:S(2)}) async-start(bf16[64,64,128]{2,1,0:T(8,128)(2,1)} %stack.2), calls=%async_computation | async-start | bytes 2097152 | tf_op jit(solution)/shard_map/all_to_all | solution.py:30
  25.8 6.5 %copy-start.4 = (bf16[256,128]{1,0:T(8,128)(2,1)S(1)}, bf16[256,128]{1,0:T(8,128)(2,1)}, u32[]{:S(2)}) copy-start(bf16[256,128]{1,0:T(8,128)(2,1)} %constant.22) | copy-start | bytes 196612
  25.8 308.1 %reduce-scatter.2.cloned.1.call-start = ((), (), s32[]{:S(2)}) async-start(), calls=%async_computation.2 | async-start | bytes 2129920 | tf_op jit(solution)/shard_map/reduce_scatter | solution.py:57
  27.5 5.4 %copy-start.3 = (bf16[256,128]{1,0:T(8,128)(2,1)S(1)}, bf16[256,128]{1,0:T(8,128)(2,1)}, u32[]{:S(2)}) copy-start(bf16[256,128]{1,0:T(8,128)(2,1)} %constant.20) | copy-start | bytes 196612
  27.5 44.6 %collective-permute-start = (bf16[128,4096]{1,0:T(8,128)(2,1)S(1)}, bf16[128,4096]{1,0:T(8,128)(2,1)S(1)}, u32[]{:S(2)}, u32[]{:S(2)}) collective-permute-start(bf16[128,4096]{1,0:T(8,128)(2,1)S(1)} %fusion.13), channel_id=1, source_target_pairs={{1,0},{2,1},{3,2},{4,3},{5,4},{6,5},{7,6},{8,7},{9,8},{10,9},{11,1... | collective-permute-start | bytes 3145736 | tf_op jit(solution)/shard_map/ppermute | solution.py:35
  34.4 37.8 %copy-start.7 = (bf16[256,128]{1,0:T(8,128)(2,1)S(1)}, bf16[256,128]{1,0:T(8,128)(2,1)}, u32[]{:S(2)}) copy-start(bf16[256,128]{1,0:T(8,128)(2,1)} %constant.21) | copy-start | bytes 196612
  37.1 35.8 %copy-start.6 = (bf16[256,128]{1,0:T(8,128)(2,1)S(1)}, bf16[256,128]{1,0:T(8,128)(2,1)}, u32[]{:S(2)}) copy-start(bf16[256,128]{1,0:T(8,128)(2,1)} %constant.23) | copy-start | bytes 196612
  76.3 3.4 copy-start.2
  89.5 2.5 copy-start.1
Sparse Core Ops, SparseCore 0:
  89.7 244.1 reduce-scatter.1
